TPU v7x, 32 devices: a whole 2x2x4 slice. The times are simulated.
32 devices in a mesh: grp: 2 (over y), frm: 4 (over z), row: 4 (over x, core).
Axes of the slice: x: 2, y: 2, z: 4, core: 2. Of those that a mesh axis runs over, the one named last changes fastest.
Arguments:
- hidden_in: bfloat16 [512, 16, 2240], P('row', ('grp', 'frm')), parts along dimension 1, may hold values from -6 to 6
- norm_gain: float32 [2240], replicated, may hold values from 0.1 to 1.9
- query_key_value_weight: bfloat16 [2240, 3, 2240], P(None, None, 'row'), may hold values from -0.125 to 0.125
- head_gain: float32 [2240], P('row'), may hold values from 0.1 to 1.9
- output_matrix: bfloat16 [2240, 2240], P('row'), may hold values from -0.125 to 0.125
- block_end: int32 [16], P(('grp', 'frm')), parts along dimension 0, may hold values from 0 to 7, as said below
Outputs:
- mixed_out: bfloat16 [512, 16, 2240], P('row', ('grp', 'frm')), parts along dimension 1
There are 2 independent parts, one for each index of `grp`. A program takes and returns all parts, laid end to end along the dimension named above; an argument that names none is the same for every part. Nothing has to cross between parts.
Inputs may be any that keep to these rules, and one draw needn't show every extreme that they name: `block_end`: entries never fall from one frame to the next; each entry is at least its frame's index, and frames with equal entries form a block of consecutive frames; a block never holds frames of two different runs of 2 frames (f // 2 differs), and the last frame of every such run ends a block.
All inputs are finite; a program needn't handle non-finite values.
Results may differ from a plain program's by a relative error of at most 0.015.
Values may be sent and summed in bfloat16 or wider, within the bound.
A program may use at most 64 MiB of HBM per device.

v0:
```python
import jax
import jax.numpy as jnp
from jax import lax
from jax.sharding import PartitionSpec as P

HD = 112


epsilon = 1e-06


def per_device(hidden_in, norm_gain, query_key_value_weight, head_gain, output_matrix, block_end):
    slab_rows, own_frames, model_width = hidden_in.shape
    local_heads = head_gain.shape[0] // HD
    group_width = local_heads * HD
    as_float = hidden_in.astype(jnp.float32)
    mean_square = jnp.mean(as_float * as_float, axis=-1, keepdims=True)
    normed = (as_float * lax.rsqrt(mean_square + epsilon) * norm_gain).astype(jnp.bfloat16)
    weights = query_key_value_weight.reshape(model_width, 3 * group_width)
    rows_per_block = lax.all_gather(normed, "row", axis=0, tiled=True)
    flat = rows_per_block.reshape(-1, model_width)
    result = jnp.dot(flat, weights, preferred_element_type=jnp.float32).astype(jnp.bfloat16)
    projected = result.reshape(rows_per_block.shape[0], own_frames, 3 * group_width)
    projected = projected.reshape(-1, own_frames, 3, local_heads, HD)
    queries = jax.nn.relu(projected[:, :, 0])
    key_relu = jax.nn.relu(projected[:, :, 1])
    values = projected[:, :, 2]
    per_frame_state = jnp.einsum(
        "pfhi,pfhj->fhij", key_relu, values, preferred_element_type=jnp.float32
    )
    per_device_sum = jnp.sum(per_frame_state, axis=0)
    earlier_mask = (block_end[None, :] <= block_end[:, None]).astype(jnp.float32)
    inside = jnp.einsum(
        "fg,ghij->fhij", earlier_mask, per_frame_state, precision=lax.Precision.HIGHEST
    )
    my_index = lax.axis_index("frm")
    rows_per_block = lax.all_gather(
        per_device_sum[None].astype(jnp.bfloat16), "frm", axis=0, tiled=True
    ).astype(jnp.float32)
    owners = jnp.arange(rows_per_block.shape[0], dtype=jnp.int32)
    include = (owners < my_index).astype(jnp.float32)
    prior_frames_sum = jnp.zeros_like(per_device_sum) + jnp.einsum(
        "n,nhij->hij", include, rows_per_block, precision=lax.Precision.HIGHEST
    )
    block_state = (inside + prior_frames_sum[None]).astype(jnp.bfloat16)
    attended = jnp.einsum(
        "pfhi,fhij->pfhj", queries, block_state, preferred_element_type=jnp.float32
    )
    head_square = jnp.mean(attended * attended, axis=-1, keepdims=True)
    head_out = (
        attended * lax.rsqrt(head_square + epsilon) * head_gain.reshape(local_heads, HD)
    ).astype(jnp.bfloat16)
    merged_heads = head_out.reshape(head_out.shape[0], own_frames, group_width)
    own_tokens = lax.all_to_all(merged_heads, "row", split_axis=0, concat_axis=2, tiled=True)
    rows_per_block = lax.all_gather(output_matrix, "row", axis=0, tiled=True)
    shards = rows_per_block.shape[0] // group_width
    split_cols = own_tokens.reshape(slab_rows, own_frames, shards, group_width)
    split_rows = rows_per_block.reshape(shards, group_width, model_width)
    products = jnp.einsum(
        "pfkc,kcd->kpfd", split_cols, split_rows, preferred_element_type=jnp.float32
    )
    rounded = lax.optimization_barrier(products.astype(jnp.bfloat16)).astype(jnp.float32)
    summed = jnp.sum(rounded, axis=0)
    return summed.astype(jnp.bfloat16)


def solution(mesh):
    placed = (
        P("row", ("grp", "frm"), None),
        P(),
        P(None, None, "row"),
        P("row"),
        P("row", None),
        P(("grp", "frm")),
    )
    return jax.shard_map(
        per_device,
        mesh=mesh,
        in_specs=placed,
        out_specs=P("row", ("grp", "frm"), None),
        check_vma=False,
    )
```

profile of v0, /device:TPU:28, one launch (start us, length us, event | category | flops | bytes accessed | tf_op | source)
XLA Modules:
  0.0 182.5 jit_solution(13249381109375235139)
XLA Ops:
  6.5 0.0 all-gather.4.cloned.1.call-start
  6.5 1.6 fusion
  8.1 2.6 %fusion.2 = bf16[128,2,2240]{0,2,1:T(8,128)(2,1)} fusion(bf16[128,2,2240]{0,2,1:T(8,128)(2,1)} %param.6, f32[2240]{0:T(1024)} %param.7, f32[128,2]{0,1:T(2,128)S(1)} %add_rsqrt_fusion.1), kind=kLoop, calls=%fused_computation.6 | loop fusion | flops 2293760 | bytes 2303744 | tf_op jit(solution)/shard_map/convert_element_type | solution.py:18
  10.8 0.0 copy-start
  10.8 0.0 all-gather.4.cloned.1.call-update
  10.8 0.0 all-gather.6.cloned.1.call-start
  10.8 0.7 all-gather.6.cloned.1.call-update
  11.5 0.0 copy-done
  11.6 0.1 mul.48
  11.6 37.6 %all-gather.4.cloned.1.call-done = bf16[512,2,2240]{0,2,1:T(8,128)(2,1)} async-done(((bf16[128,2,2240]{0,2,1:T(8,128)(2,1)}), bf16[512,2,2240]{0,2,1:T(8,128)(2,1)}) %all-gather.4.cloned.1.call-update) | async-done | bytes 4587536 | tf_op jit(solution)/shard_map/all_gather | solution.py:20
  49.2 12.7 %copy.16 = bf16[512,2,2240]{2,1,0:T(2,128)(2,1)} copy(bf16[512,2,2240]{0,2,1:T(8,128)(2,1)} %all-gather.4.cloned.1.call-done) | data formatting | bytes 9175040 | tf_op jit(solution)/shard_map/all_gather | solution.py:20
  61.9 10.8 %reshape.48 = bf16[1024,2240]{1,0:T(8,128)(2,1)} reshape(bf16[512,2,2240]{2,1,0:T(2,128)(2,1)} %copy.16) | data formatting | bytes 9175040 | tf_op jit(solution)/shard_map/reshape | solution.py:21
  72.7 11.9 %convolution_convert_fusion.1 = bf16[1024,1680]{0,1:T(8,128)(2,1)S(1)} fusion(bf16[1024,2240]{1,0:T(8,128)(2,1)} %reshape.48, bf16[2240,1680]{0,1:T(8,128)(2,1)} %bitcast.55), kind=kOutput, calls=%fused_computation.1 | convolution fusion | flops 7708753920 | bytes 15554560 | tf_op jit(solution)/shard_map/dot_general | solution.py:22
  84.7 3.8 %copy.17 = bf16[1024,1680]{1,0:T(8,128)(2,1)} copy(bf16[1024,1680]{0,1:T(8,128)(2,1)S(1)} %convolution_convert_fusion.1) | data formatting | bytes 6881280 | tf_op jit(solution)/shard_map/convert_element_type | solution.py:22
  88.4 11.4 %reshape_reshape.3 = bf16[512,2,3,5,112]{4,3,2,1,0:T(8,128)(2,1)} reshape(bf16[1024,1680]{1,0:T(8,128)(2,1)} %copy.17) | data formatting | bytes 6881280 | tf_op jit(solution)/shard_map/reshape;reshape | solution.py:24
  99.8 5.9 %fusion.29 = (bf16[512,2,1,5,112]{4,3,2,1,0:T(8,128)(2,1)}, bf16[512,2,1,5,112]{4,3,2,1,0:T(8,128)(2,1)}, bf16[512,2,1,5,112]{4,3,2,1,0:T(8,128)(2,1)S(1)}) fusion(bf16[512,2,3,5,112]{4,3,2,1,0:T(8,128)(2,1)} %reshape_reshape.3), kind=kLoop, calls=%fused_computation.39 | loop fusion | bytes 6881280 | tf_op jit(solution)/shard_map/slice | solution.py:26
  105.8 4.1 %copy.33 = bf16[512,2,1,5,112]{0,4,3,1,2:T(8,128)(2,1)} copy(bf16[512,2,1,5,112]{4,3,2,1,0:T(8,128)(2,1)} %get-tuple-element.5) | data formatting | bytes 2293760
  109.8 4.1 %copy.34 = bf16[512,2,1,5,112]{0,4,3,1,2:T(8,128)(2,1)} copy(bf16[512,2,1,5,112]{4,3,2,1,0:T(8,128)(2,1)} %get-tuple-element.6) | data formatting | bytes 2293760
  113.9 1.4 copy.35
  115.3 0.0 copy-start.1
  115.3 2.1 %fusion.30 = (bf16[5,112,112]{2,1,0:T(8,128)(2,1)S(1)}, f32[2,5,112,112]{3,2,1,0:T(8,128)S(1)}) fusion(bf16[512,2,1,5,112]{0,4,3,1,2:T(8,128)(2,1)} %copy.34, bf16[512,2,1,5,112]{0,4,3,1,2:T(8,128)(2,1)} %copy.33), kind=kOutput, calls=%fused_computation.40 | convolution fusion | flops 129086720 | bytes 2920960 | tf_op jit(solution)/shard_map/pfhi,pfhj->fhij/dot_general | solution.py:28
  117.4 16.8 %all-gather = bf16[20,112,112]{2,1,0:T(8,128)(2,1)S(1)} all-gather(bf16[5,112,112]{2,1,0:T(8,128)(2,1)S(1)} %get-tuple-element.8), channel_id=2, replica_groups=mesh['grp'=2,'frm'=4,'row'=4] {'frm'}, dimensions={0}, use_global_device_ids=true | all-gather | bytes 627200 | tf_op jit(solution)/shard_map/all_gather | solution.py:37
  134.2 0.4 fusion.18
  134.6 0.0 copy-done.1
  134.7 1.5 fusion.6
  136.1 0.5 fusion.3
  136.7 0.3 fusion.5
  137.0 1.9 %copy.23 = bf16[512,2,560]{2,1,0:T(2,128)(2,1)S(1)} copy(bf16[512,2,560]{0,2,1:T(8,128)(2,1)S(1)} %bitcast.52) | data formatting | bytes 2293760 | tf_op jit(solution)/shard_map/reshape | solution.py:53
  138.9 19.7 %all_to_all.15 = bf16[512,2,560]{2,1,0:T(2,128)(2,1)S(1)} all-to-all(bf16[512,2,560]{2,1,0:T(2,128)(2,1)S(1)} %copy.23), channel_id=1, replica_groups=mesh['grp'=2,'frm'=4,'row'=4] {'row'}, dimensions={0} | all-to-all | bytes 2293760 | tf_op jit(solution)/shard_map/all_to_all | solution.py:54
  158.6 2.0 %copy.25 = bf16[4,128,2,560]{1,3,2,0:T(8,128)(2,1)S(1)} copy(bf16[4,128,2,560]{3,2,1,0:T(2,128)(2,1)S(1)} %bitcast.51) | data formatting | bytes 2293760 | tf_op jit(solution)/shard_map/all_to_all | solution.py:54
  160.6 0.0 all-gather.6.cloned.1.call-done
  160.6 10.8 %convolution_convert_fusion = bf16[4,128,2,2240]{1,3,2,0:T(8,128)(2,1)} fusion(bf16[4,560,2240,1]{2,1,3,0:T(8,128)(2,1)} %bitcast.54, bf16[4,128,2,560]{1,3,2,0:T(8,128)(2,1)S(1)} %copy.25), kind=kOutput, calls=%fused_computation | convolution fusion | flops 2571304960 | bytes 15769600 | tf_op jit(solution)/shard_map/pfkc,kcd->kpfd/dot_general | solution.py:59
  171.4 4.3 %reduce_sum.42 = bf16[128,2,2240]{0,2,1:T(8,128)(2,1)} reduce(bf16[4,128,2,2240]{1,3,2,0:T(8,128)(2,1)} %convolution_convert_fusion, bf16[]{:T(256)} %constant.17.clone.1), dimensions={0}, to_apply=%region_3.4 | reduce | flops 1720320 | bytes 5734402 | tf_op jit(solution)/shard_map/reduce_sum | solution.py:63
  (2 shorter events, 0.0 us)
Async XLA Ops:
  6.5 42.6 %all-gather.4.cloned.1.call-start = ((), (), s32[]{:S(2)}) async-start(), calls=%async_computation.1 | async-start | bytes 5734400 | tf_op jit(solution)/shard_map/all_gather | solution.py:20
  10.8 0.8 copy-start
  10.8 149.8 %all-gather.6.cloned.1.call-start = ((), (), s32[]{:S(2)}) async-start(), calls=%async_computation.2 | async-start | bytes 12902400 | tf_op jit(solution)/shard_map/all_gather | solution.py:55
  115.3 19.3 %copy-start.1 = (s32[2]{0:T(128)S(1)}, s32[2]{0:T(128)}, u32[]{:S(2)}) copy-start(s32[2]{0:T(128)} %param.11) | copy-start | bytes 28
Sparse Core Ops, SparseCore 0:
  10.9 38.2 all-gather.3
  50.7 69.2 all-gather.5
where the time goes:
time: 186 us; the launch traced here: 183 us
  local copies, waits for them, and re-layouts  58.2 us (31%)
  waiting for transfers between devices  38.3 us (21%)
  blocking collectives  36.5 us (20%)
  matrix products  27.2 us (15%)
  between operations  13.5 us (7%)
  other arithmetic  8.82 us (5%)
    all_gather x1, waiting for transfers between devices, per_device(): rows_per_block = lax.all_gather(normed, 'row', axis=0, tiled=True)  37.6 us
    all_to_all x1, blocking collectives, per_device(): lax.all_to_all(merged_heads, 'row', split_axis=0, concat_axis=2, tiled=True)  19.7 us
    all_gather x1, blocking collectives, per_device(): lax.all_gather(per_device_sum[None].astype(jnp.bfloat16), 'frm', axis=0,...  16.8 us
    all_gather x1, local copies, waits for them, and re-layouts, per_device(): rows_per_block = lax.all_gather(normed, 'row', axis=0, tiled=True)  12.7 us
    dot_general x1, matrix products, per_device(): jnp.dot(flat, weights, preferred_element_type=jnp.float32)  11.9 us
    another operation x1, local copies, waits for them, and re-layouts, per_device(): projected = projected.reshape(-1, own_frames, 3, local_heads, HD)  11.4 us
    reshape x1, local copies, waits for them, and re-layouts, per_device(): flat = rows_per_block.reshape(-1, model_width)  10.8 us
    dot_general x1, matrix products, per_device(): jnp.einsum('pfkc,kcd->kpfd', split_cols, split_rows, preferred_element_ty...  10.8 us
  transfers between devices with their start and end apart: 2, of which 1 were waited for; matrix products, arithmetic and copies ran while one was open for 41% of the time, Pallas kernels for 0%

commit v1 on v0

v1 whole, which is shorter than its diff:
```python
import functools

import jax
import jax.numpy as jnp
from jax import lax
from jax.experimental import pallas as pl
from jax.experimental.pallas import tpu as pltpu
from jax.sharding import PartitionSpec as P

HD = 112
LANES = 128
PARTS = 3
QUERY, KEY, VALUE = 0, 1, 2

epsilon = 1e-06


def slices_of(rows, wanted):
    count = wanted
    while rows % count or (rows // count) % 16:
        count -= 1
    return count, rows // count


def kernel(
    n_row, n_frm,
    hid, ng, w_hbm, hg, wo_hbm, block_end,
    out,
    xg, w, wo, wot, proj, st, chain_s, prior, ho_c, ho_o, hs_c, hs_o, red_s, red_r,
    w_sem, wo_sem, wx_s, wx_r, gp_s, gp_r, gx_s, gx_r, gf_s, gf_r, ch_s, ch_r, he_s, he_r, rd_s, rd_r,
):
    frames, width, slab = hid.shape
    group_width = w.shape[1]
    heads = group_width // HD
    me = lax.axis_index("row")
    fi = lax.axis_index("frm")
    mate = me + 1 - 2 * lax.rem(me, 2)
    cross = lax.rem(me + 2, n_row)

    def remote(src, dst, s, r, **where):
        return pltpu.make_async_remote_copy(
            src_ref=src, dst_ref=dst, send_sem=s, recv_sem=r,
            device_id=where, device_id_type=pl.DeviceIdType.MESH,
        )

    barrier = pltpu.get_barrier_semaphore()
    for where in (
        {"row": mate}, {"row": cross},
        {"frm": lax.rem(fi + 1, n_frm)}, {"frm": lax.rem(fi + n_frm - 1, n_frm)},
    ):
        pl.semaphore_signal(barrier, inc=1, device_id=where, device_id_type=pl.DeviceIdType.MESH)

    w_copies = {}
    for part in (KEY, VALUE, QUERY):
        w_copies[part] = pltpu.make_async_copy(w_hbm.at[part], w.at[part], w_sem.at[part])
        w_copies[part].start()
    wo_copy = pltpu.make_async_copy(wo_hbm, wo.at[pl.ds(0, group_width)], wo_sem.at[0])
    wo_copy.start()

    norm_steps, norm_rows = slices_of(width, 14)

    def norm(f):
        def squares(i, acc):
            rows = pl.ds(pl.multiple_of(i * norm_rows, 16), norm_rows)
            v = hid[f, rows, :].astype(jnp.float32)
            return acc + jnp.sum((v * v).reshape(norm_rows // 8, 8, slab), axis=0)

        acc = lax.fori_loop(0, norm_steps, squares, jnp.zeros((8, slab), jnp.float32))
        scale = lax.rsqrt(jnp.sum(acc, axis=0, keepdims=True) / width + epsilon)

        def write(i, carry):
            rows = pl.ds(pl.multiple_of(i * norm_rows, 16), norm_rows)
            v = hid[f, rows, :].astype(jnp.float32)
            xg[0, f, rows, :] = (v * scale * ng[rows, :]).astype(jnp.bfloat16)
            return carry

        lax.fori_loop(0, norm_steps, write, 0)

    to_mate, to_cross, forward = [], [], []
    for f in range(frames):
        to_mate.append(remote(xg.at[0, f], xg.at[1, f], gp_s.at[f], gp_r.at[f], row=mate))
        to_cross.append(remote(xg.at[0, f], xg.at[2, f], gx_s.at[f], gx_r.at[f], row=cross))
        forward.append(remote(xg.at[2, f], xg.at[3, f], gf_s.at[f], gf_r.at[f], row=mate))
    wo_exchange = remote(
        wo_hbm, wo.at[pl.ds(group_width, group_width)], wx_s.at[0], wx_r.at[0], row=mate
    )

    for f in range(frames):
        norm(f)
        if f == 0:
            pl.semaphore_wait(barrier, 4)
        to_cross[f].start()
        to_mate[f].start()
    wo_exchange.start()

    def project(f, first, part):
        tokens = jnp.concatenate([xg[first, f], xg[first + 1, f]], axis=1)
        r = jnp.dot(w[part], tokens, preferred_element_type=jnp.float32)
        if part != VALUE:
            r = jnp.maximum(r, 0.0)
        proj[f, part, :, pl.ds(first * slab, 2 * slab)] = r.astype(jnp.bfloat16)

    def add_state(f, first):
        for h in range(heads):
            rows, cols = pl.ds(h * HD, HD), pl.ds(first * slab, 2 * slab)
            s = lax.dot_general(
                proj[f, VALUE, rows, cols], proj[f, KEY, rows, cols],
                (((1,), (1,)), ((), ())), preferred_element_type=jnp.float32,
            )
            if first == 0:
                st[f, h] = s
            else:
                st[f, h] += s

    for f in range(frames):
        to_mate[f].wait_recv()
        for part in (KEY, VALUE, QUERY):
            if f == 0:
                w_copies[part].wait()
            project(f, 0, part)
        add_state(f, 0)

    def transpose_rows(start, count):
        wot[:, pl.ds(start, count)] = wo[pl.ds(start, count), :].T

    wo_copy.wait()
    wo_exchange.wait_recv()

    def flip(i, carry):
        rows = pl.ds(pl.multiple_of(i * LANES, LANES), LANES)
        wot[:, rows] = wo[rows, :].T
        return carry

    whole = 2 * group_width // LANES
    lax.fori_loop(0, whole, flip, 0)
    if 2 * group_width % LANES:
        transpose_rows(whole * LANES, 2 * group_width % LANES)

    for f in range(frames):
        to_cross[f].wait_recv()
        forward[f].start()
        forward[f].wait_recv()
        project(f, 2, KEY)
        project(f, 2, VALUE)
        if f < frames - 1:
            project(f, 2, QUERY)
        add_state(f, 2)

    chain = [
        remote(chain_s.at[h], prior.at[h], ch_s.at[h], ch_r.at[h], frm=lax.rem(fi + 1, n_frm))
        for h in range(heads)
    ]

    def own_sum(h):
        total = st[0, h]
        for f in range(1, frames):
            total = total + st[f, h]
        return total

    @pl.when(fi == 0)
    def _():
        for h in range(heads):
            chain_s[h] = own_sum(h).astype(jnp.bfloat16)
            chain[h].start()
        prior[...] = jnp.zeros_like(prior)

    project(frames - 1, 2, QUERY)

    @pl.when(fi > 0)
    def _():
        for h in range(heads):
            chain[h].wait_recv()

            @pl.when(fi < n_frm - 1)
            def _():
                chain_s[h] = (prior[h].astype(jnp.float32) + own_sum(h)).astype(jnp.bfloat16)
                chain[h].start()

    def attend(first, keep, give):
        cols = pl.ds(first * slab, 2 * slab)
        for f in range(frames):
            for h in range(heads):
                rows = pl.ds(h * HD, HD)
                total = prior[h].astype(jnp.float32)
                for g in range(frames):
                    use = jnp.where(block_end[g] <= block_end[f], 1.0, 0.0)
                    total = total + use * st[g, h]
                a = jnp.dot(
                    total.astype(jnp.bfloat16), proj[f, QUERY, rows, cols],
                    preferred_element_type=jnp.float32,
                )
                scale = lax.rsqrt(jnp.mean(a * a, axis=0, keepdims=True) + epsilon)
                a = a * scale
                gain = hg[rows, :]
                keep[rows, pl.ds(f * slab, slab)] = (a[:, :slab] * gain).astype(jnp.bfloat16)
                give[rows, pl.ds(f * slab, slab)] = (a[:, slab:] * gain).astype(jnp.bfloat16)

    swap_c = remote(hs_c, ho_c.at[pl.ds(group_width, group_width)], he_s.at[0], he_r.at[0], row=mate)
    swap_o = remote(hs_o, ho_o.at[pl.ds(group_width, group_width)], he_s.at[1], he_r.at[1], row=mate)
    attend(2, ho_c, hs_c)
    swap_c.start()
    attend(0, ho_o, hs_o)
    swap_o.start()
    swap_c.wait_recv()

    n_red = rd_s.shape[0]
    red_rows = width // n_red
    reduce = []
    for i in range(n_red):
        rows = pl.ds(i * red_rows, red_rows)
        r = jnp.dot(wot[rows, :], ho_c[...], preferred_element_type=jnp.float32)
        for f in range(frames):
            red_s[f, rows, :] = r[:, f * slab:(f + 1) * slab].astype(jnp.bfloat16)
        reduce.append(remote(
            red_s.at[:, rows, :], red_r.at[:, rows, :], rd_s.at[i], rd_r.at[i], row=cross
        ))
        reduce[i].start()

    swap_o.wait_recv()
    for i in range(n_red):
        rows = pl.ds(i * red_rows, red_rows)
        r = jnp.dot(wot[rows, :], ho_o[...], preferred_element_type=jnp.float32)
        reduce[i].wait_recv()
        for f in range(frames):
            other = red_r[f, rows, :].astype(jnp.float32)
            out[f, rows, :] = (r[:, f * slab:(f + 1) * slab] + other).astype(jnp.bfloat16)

    for copy in to_mate + to_cross + forward + [wo_exchange, swap_c, swap_o] + reduce:
        copy.wait_send()

    @pl.when(fi < n_frm - 1)
    def _():
        for h in range(heads):
            chain[h].wait_send()


def per_device(n_row, n_frm, hidden_in, norm_gain, query_key_value_weight, head_gain, output_matrix, block_end):
    slab, frames, width = hidden_in.shape
    group_width = head_gain.shape[0]
    heads = group_width // HD
    bf16, f32 = jnp.bfloat16, jnp.float32
    n_red, _ = slices_of(width, 5)
    vmem = pl.BlockSpec(memory_space=pltpu.VMEM)
    hbm = pl.BlockSpec(memory_space=pl.ANY)
    smem = pl.BlockSpec(memory_space=pltpu.SMEM)
    dma = pltpu.SemaphoreType.DMA
    result = pl.pallas_call(
        functools.partial(kernel, n_row, n_frm),
        out_shape=jax.ShapeDtypeStruct((frames, width, slab), bf16),
        in_specs=[vmem, vmem, hbm, vmem, hbm, smem],
        out_specs=vmem,
        scratch_shapes=[
            pltpu.VMEM((n_row, frames, width, slab), bf16),
            pltpu.VMEM((PARTS, group_width, width), bf16),
            pltpu.VMEM((2 * group_width, width), bf16),
            pltpu.VMEM((width, 2 * group_width), bf16),
            pltpu.VMEM((frames, PARTS, group_width, n_row * slab), bf16),
            pltpu.VMEM((frames, heads, HD, HD), f32),
            pltpu.VMEM((heads, HD, HD), bf16),
            pltpu.VMEM((heads, HD, HD), bf16),
            pltpu.VMEM((2 * group_width, frames * slab), bf16),
            pltpu.VMEM((2 * group_width, frames * slab), bf16),
            pltpu.VMEM((group_width, frames * slab), bf16),
            pltpu.VMEM((group_width, frames * slab), bf16),
            pltpu.VMEM((frames, width, slab), bf16),
            pltpu.VMEM((frames, width, slab), bf16),
            dma((PARTS,)), dma((1,)), dma((1,)), dma((1,)),
            dma((frames,)), dma((frames,)), dma((frames,)), dma((frames,)),
            dma((frames,)), dma((frames,)),
            dma((heads,)), dma((heads,)), dma((2,)), dma((2,)),
            dma((n_red,)), dma((n_red,)),
        ],
        compiler_params=pltpu.CompilerParams(
            collective_id=0, has_side_effects=True, vmem_limit_bytes=60 * 1024 * 1024
        ),
        name="layer",
    )(
        hidden_in.transpose(1, 2, 0),
        jnp.broadcast_to(norm_gain[:, None], (width, slab)),
        query_key_value_weight.transpose(1, 2, 0),
        jnp.broadcast_to(head_gain[:, None], (group_width, slab)),
        output_matrix,
        block_end,
    )
    return result.transpose(2, 0, 1)


def solution(mesh):
    placed = (
        P("row", ("grp", "frm"), None),
        P(),
        P(None, None, "row"),
        P("row"),
        P("row", None),
        P(("grp", "frm")),
    )
    return jax.shard_map(
        functools.partial(per_device, mesh.shape["row"], mesh.shape["frm"]),
        mesh=mesh,
        in_specs=placed,
        out_specs=P("row", ("grp", "frm"), None),
        check_vma=False,
    )
```

time: 186 us -> 79.7 us (0.43); the launches traced: 183 us -> 79.4 us
  Pallas kernels: 0 us -> 73.5 us
  local copies, waits for them, and re-layouts: 58.2 us -> 5.94 us
  waiting for transfers between devices: 38.3 us -> 0 us
  blocking collectives: 36.5 us -> 0 us
  matrix products: 27.2 us -> 0 us
  between operations: 13.5 us -> 0.01 us
  other arithmetic: 8.82 us -> 0 us
    pallas_call x0 -> x1, Pallas kernels: none -> 73.5 us  [per_device(): pl.pallas_call(functools.partial(kernel, n_row, n_frm), out_shape=jax.Sha...]
    all_gather x2 -> x0, waiting for transfers between devices: 37.6 us -> none  [the longest x1 37.6 us: per_device(): rows_per_block = lax.all_gather(normed, 'row', axis=0, tiled=True)]
    dot_general x6 -> x0, matrix products: 27.2 us -> none  [the longest x1 11.9 us: per_device(): jnp.dot(flat, weights, preferred_element_type=jnp.float32)]
    all_to_all x1 -> x0, blocking collectives: 19.7 us -> none  [per_device(): lax.all_to_all(merged_heads, 'row', split_axis=0, concat_axis=2, tiled=True)]
    all_gather x1 -> x0, blocking collectives: 16.8 us -> none  [per_device(): lax.all_gather(per_device_sum[None].astype(jnp.bfloat16), 'frm', axis=0,...]
    all_gather x1 -> x0, local copies, waits for them, and re-layouts: 12.7 us -> none  [per_device(): rows_per_block = lax.all_gather(normed, 'row', axis=0, tiled=True)]
    reshape x2 -> x0, local copies, waits for them, and re-layouts: 12.7 us -> none  [the longest x1 10.8 us: per_device(): flat = rows_per_block.reshape(-1, model_width)]
    another operation x1 -> x0, local copies, waits for them, and re-layouts: 11.4 us -> none  [per_device(): projected = projected.reshape(-1, own_frames, 3, local_heads, HD)]
  transfers between devices with their start and end apart: 2 -> 0, of which waited for: 1 -> 0; matrix products, arithmetic and copies ran while one was open for 41% -> 0% of each run, Pallas kernels for 0% -> 0%
where the time goes in v1:
time: 79.7 us; the launch traced here: 79.4 us
  Pallas kernels  73.5 us (92%)
  local copies, waits for them, and re-layouts  5.94 us (7%)
    pallas_call x1, Pallas kernels, per_device(): pl.pallas_call(functools.partial(kernel, n_row, n_frm), out_shape=jax.Sha...  73.5 us
    unnamed x1, local copies, waits for them, and re-layouts  2.34 us
    broadcast_in_dim x1, local copies, waits for them, and re-layouts, per_device(): jnp.broadcast_to(norm_gain[:, None], (width, slab))  2.07 us

profile of v1, /device:TPU:28, one launch (start us, length us, event | category | flops | bytes accessed | tf_op | source)
XLA Modules:
  0.0 79.4 jit_solution(5198572545011805196)
XLA Ops:
  0.0 1.5 %broadcast_in_dim.5.hg = f32[560,128]{1,0:T(8,128)} broadcast(f32[560]{0:T(1024)} %param.9), dimensions={0} | broadcast | bytes 288960 | tf_op jit(solution)/shard_map/broadcast_in_dim | solution.py:281
  1.5 2.1 %broadcast_in_dim.4.ng = f32[2240,128]{1,0:T(8,128)} broadcast(f32[2240]{0:T(1024)} %param.7), dimensions={0} | broadcast | bytes 1155840 | tf_op jit(solution)/shard_map/broadcast_in_dim | solution.py:279
  3.6 73.5 %layer.1 = bf16[2,2240,128]{2,1,0:T(8,128)(2,1)} custom-call(bf16[2,2240,128]{2,1,0:T(8,128)(2,1)} %bitcast.5, f32[2240,128]{1,0:T(8,128)} %broadcast_in_dim.4.ng, bf16[3,560,2240]{2,1,0:T(8,128)(2,1)} %bitcast.3, f32[560,128]{1,0:T(8,128)} %broadcast_in_dim.5.hg, bf16[560,2240]{1,0:T(8,128)(2,1)} %wo_hbm.1, s32[2]{0:T(128)} %block_end.1), custom_call_target="tpu_custom_call" | custom-call | tf_op jit(solution)/shard_map/layer/pallas_call | solution.py:247
  77.1 2.3 %copy.8 = bf16[128,2,2240]{0,2,1:T(8,128)(2,1)} copy(bf16[128,2,2240]{0,2,1:T(8,128)(2,1)} %bitcast.4) | data formatting | bytes 2293760

commit v2 on v1

--- a/solution.py
+++ b/solution.py
@@ -26,7 +26,7 @@
     n_row, n_frm,
     hid, ng, w_hbm, hg, wo_hbm, block_end,
     out,
-    xg, w, wo, wot, proj, st, chain_s, prior, ho_c, ho_o, hs_c, hs_o, red_s, red_r,
+    ng_c, hg_c, xg, w, wo, wot, proj, st, chain_s, prior, ho_c, ho_o, hs_c, hs_o, red_s, red_r,
     w_sem, wo_sem, wx_s, wx_r, gp_s, gp_r, gx_s, gx_r, gf_s, gf_r, ch_s, ch_r, he_s, he_r, rd_s, rd_r,
 ):
     frames, width, slab = hid.shape
@@ -57,6 +57,13 @@
     wo_copy = pltpu.make_async_copy(wo_hbm, wo.at[pl.ds(0, group_width)], wo_sem.at[0])
     wo_copy.start()
 
+    def as_column(row, column):
+        for start in range(0, column.shape[0], LANES):
+            count = min(LANES, column.shape[0] - start)
+            spread = jnp.broadcast_to(row[:, pl.ds(start, count)], (LANES, count))
+            column[pl.ds(start, count), :] = spread.T
+
+    as_column(ng, ng_c)
     norm_steps, norm_rows = slices_of(width, 14)
 
     def norm(f):
@@ -71,16 +78,23 @@
         def write(i, carry):
             rows = pl.ds(pl.multiple_of(i * norm_rows, 16), norm_rows)
             v = hid[f, rows, :].astype(jnp.float32)
-            xg[0, f, rows, :] = (v * scale * ng[rows, :]).astype(jnp.bfloat16)
+            xg[0, f, rows, :] = (v * scale * ng_c[rows, :]).astype(jnp.bfloat16)
             return carry
 
         lax.fori_loop(0, norm_steps, write, 0)
 
     to_mate, to_cross, forward = [], [], []
+    n_cut, cut_rows = slices_of(width, 4)
     for f in range(frames):
         to_mate.append(remote(xg.at[0, f], xg.at[1, f], gp_s.at[f], gp_r.at[f], row=mate))
-        to_cross.append(remote(xg.at[0, f], xg.at[2, f], gx_s.at[f], gx_r.at[f], row=cross))
-        forward.append(remote(xg.at[2, f], xg.at[3, f], gf_s.at[f], gf_r.at[f], row=mate))
+        for k in range(n_cut):
+            rows, i = pl.ds(k * cut_rows, cut_rows), f * n_cut + k
+            to_cross.append(remote(
+                xg.at[0, f, rows], xg.at[2, f, rows], gx_s.at[i], gx_r.at[i], row=cross
+            ))
+            forward.append(remote(
+                xg.at[2, f, rows], xg.at[3, f, rows], gf_s.at[i], gf_r.at[i], row=mate
+            ))
     wo_exchange = remote(
         wo_hbm, wo.at[pl.ds(group_width, group_width)], wx_s.at[0], wx_r.at[0], row=mate
     )
@@ -89,7 +103,8 @@
         norm(f)
         if f == 0:
             pl.semaphore_wait(barrier, 4)
-        to_cross[f].start()
+        for k in range(n_cut):
+            to_cross[f * n_cut + k].start()
         to_mate[f].start()
     wo_exchange.start()
 
@@ -123,6 +138,7 @@
     def transpose_rows(start, count):
         wot[:, pl.ds(start, count)] = wo[pl.ds(start, count), :].T
 
+    as_column(hg, hg_c)
     wo_copy.wait()
     wo_exchange.wait_recv()
 
@@ -137,9 +153,11 @@
         transpose_rows(whole * LANES, 2 * group_width % LANES)
 
     for f in range(frames):
-        to_cross[f].wait_recv()
-        forward[f].start()
-        forward[f].wait_recv()
+        for k in range(f * n_cut, (f + 1) * n_cut):
+            to_cross[k].wait_recv()
+            forward[k].start()
+        for k in range(f * n_cut, (f + 1) * n_cut):
+            forward[k].wait_recv()
         project(f, 2, KEY)
         project(f, 2, VALUE)
         if f < frames - 1:
@@ -191,7 +209,7 @@
                 )
                 scale = lax.rsqrt(jnp.mean(a * a, axis=0, keepdims=True) + epsilon)
                 a = a * scale
-                gain = hg[rows, :]
+                gain = hg_c[rows, :]
                 keep[rows, pl.ds(f * slab, slab)] = (a[:, :slab] * gain).astype(jnp.bfloat16)
                 give[rows, pl.ds(f * slab, slab)] = (a[:, slab:] * gain).astype(jnp.bfloat16)
 
@@ -239,7 +257,8 @@
     group_width = head_gain.shape[0]
     heads = group_width // HD
     bf16, f32 = jnp.bfloat16, jnp.float32
-    n_red, _ = slices_of(width, 5)
+    n_red, _ = slices_of(width, 7)
+    n_cut, _ = slices_of(width, 4)
     vmem = pl.BlockSpec(memory_space=pltpu.VMEM)
     hbm = pl.BlockSpec(memory_space=pl.ANY)
     smem = pl.BlockSpec(memory_space=pltpu.SMEM)
@@ -250,6 +269,8 @@
         in_specs=[vmem, vmem, hbm, vmem, hbm, smem],
         out_specs=vmem,
         scratch_shapes=[
+            pltpu.VMEM((width, slab), f32),
+            pltpu.VMEM((group_width, slab), f32),
             pltpu.VMEM((n_row, frames, width, slab), bf16),
             pltpu.VMEM((PARTS, group_width, width), bf16),
             pltpu.VMEM((2 * group_width, width), bf16),
@@ -265,8 +286,8 @@
             pltpu.VMEM((frames, width, slab), bf16),
             pltpu.VMEM((frames, width, slab), bf16),
             dma((PARTS,)), dma((1,)), dma((1,)), dma((1,)),
-            dma((frames,)), dma((frames,)), dma((frames,)), dma((frames,)),
             dma((frames,)), dma((frames,)),
+            *[dma((frames * n_cut,)) for _ in range(4)],
             dma((heads,)), dma((heads,)), dma((2,)), dma((2,)),
             dma((n_red,)), dma((n_red,)),
         ],
@@ -276,9 +297,9 @@
         name="layer",
     )(
         hidden_in.transpose(1, 2, 0),
-        jnp.broadcast_to(norm_gain[:, None], (width, slab)),
+        norm_gain[None, :],
         query_key_value_weight.transpose(1, 2, 0),
-        jnp.broadcast_to(head_gain[:, None], (group_width, slab)),
+        head_gain[None, :],
         output_matrix,
         block_end,
     )

time: 79.7 us -> 78.2 us (0.981)
  local copies, waits for them, and re-layouts: 5.94 us -> 4.91 us
    broadcast_in_dim x2, local copies, waits for them, and re-layouts: 3.6 us -> 2.57 us  [the longest x1 1.31 us: per_device(): norm_gain[None, :]]
where the time goes in v2:
time: 78.2 us; the launch traced here: 77.9 us
  Pallas kernels  73 us (93%)
  local copies, waits for them, and re-layouts  4.91 us (6%)
    pallas_call x1, Pallas kernels, per_device(): pl.pallas_call(functools.partial(kernel, n_row, n_frm), out_shape=jax.Sha...  73 us
    unnamed x1, local copies, waits for them, and re-layouts  2.34 us

profile of v2, /device:TPU:28, one launch (start us, length us, event | category | flops | bytes accessed | tf_op | source)
XLA Modules:
  0.0 77.9 jit_solution(367812445053330149)
XLA Ops:
  0.0 1.3 %broadcast_in_dim.7.hg = f32[1,560]{1,0:T(1,128)} reshape(f32[560]{0:T(1024)} %param.9) | data formatting | bytes 4480 | tf_op jit(solution)/shard_map/broadcast_in_dim | solution.py:302
  1.3 1.3 %broadcast_in_dim.6.ng = f32[1,2240]{1,0:T(1,128)} reshape(f32[2240]{0:T(1024)} %param.7) | data formatting | bytes 17920 | tf_op jit(solution)/shard_map/broadcast_in_dim | solution.py:300
  2.6 73.0 %layer.1 = bf16[2,2240,128]{2,1,0:T(8,128)(2,1)} custom-call(bf16[2,2240,128]{2,1,0:T(8,128)(2,1)} %bitcast.5, f32[1,2240]{1,0:T(1,128)} %broadcast_in_dim.6.ng, bf16[3,560,2240]{2,1,0:T(8,128)(2,1)} %bitcast.3, f32[1,560]{1,0:T(1,128)} %broadcast_in_dim.7.hg, bf16[560,2240]{1,0:T(8,128)(2,1)} %wo_hbm.1, s32[2]{0:T(128)} %block_end.1), custom_call_target="tpu_custom_call" | custom-call | tf_op jit(solution)/shard_map/layer/pallas_call | solution.py:266
  75.6 2.3 %copy.8 = bf16[128,2,2240]{0,2,1:T(8,128)(2,1)} copy(bf16[128,2,2240]{0,2,1:T(8,128)(2,1)} %bitcast.4) | data formatting | bytes 2293760
